TPU v7x, 512 devices: a whole 4x8x8 slice. The times are simulated.
512 devices in a mesh: tm: 16 (over z, core), space: 32 (over y, x).
Axes of the slice: x: 4, y: 8, z: 8, core: 2. Of those that a mesh axis runs over, the one named last changes fastest.
Arguments:
- thermal_anomaly_matrix: float32 [512, 393216], P('tm', 'space'), may hold values from -40 to 40
- filter_weights: float32 [31], replicated, may hold values from -0.12 to 1.2
Outputs:
- lower_factor: float32 [512, 512], replicated
- basis: float32 [512, 32, 12288], P(None, 'space', 'tm')
All inputs are finite; a program needn't handle non-finite values.
Results may differ from a plain program's by a relative error of at most 0.000078.
Values sent between devices are 32-bit elements; how exact they have to be, the bound alone decides.
A program may use at most 64 MiB of HBM per device.

v0:
```python
import jax
import jax.numpy as jnp
from jax import lax
from jax.sharding import PartitionSpec as P


def padded(array, sides, width):
    for axis, dim in sides:
        size, length = (lax.axis_size(axis), array.shape[dim])
        up = [(i, (i + 1) % size) for i in range(size - 1)]
        down = [(j, i) for i, j in up]
        last = lax.slice_in_dim(array, length - width, length, axis=dim)
        initial = lax.slice_in_dim(array, 0, width, axis=dim)
        before = lax.ppermute(last, axis, up)
        after = lax.ppermute(initial, axis, down)
        array = jnp.concatenate([before, array, after], axis=dim)
    return array


def apply_filter_weights(boundary_extended_record, filter_weights, length):
    summed = jnp.zeros((length, boundary_extended_record.shape[1]), jnp.float32)
    for offset in range(filter_weights.shape[0]):
        summed = (
            summed + filter_weights[offset] * boundary_extended_record[offset : offset + length]
        )
    return summed


def resample_grid_points(slab):
    return lax.all_to_all(slab, "tm", split_axis=1, concat_axis=0, tiled=True)


def per_device(thermal_anomaly_matrix, filter_weights):
    stencil_radius = (filter_weights.shape[0] - 1) // 2
    boundary_extended_record = padded(thermal_anomaly_matrix, (("tm", 0),), stencil_radius)
    lowpassed_record = resample_grid_points(
        apply_filter_weights(
            boundary_extended_record, filter_weights, thermal_anomaly_matrix.shape[0]
        )
    )
    local_gram = lax.dot_general(
        lowpassed_record,
        lowpassed_record,
        (((1,), (1,)), ((), ())),
        precision=lax.Precision.HIGHEST,
        preferred_element_type=jnp.float32,
    )
    gram_matrix = lax.psum(local_gram, ("tm", "space"))
    point_count = lowpassed_record.shape[1] * lax.axis_size("tm") * lax.axis_size("space")
    gram_matrix = gram_matrix / jnp.float32(point_count)
    lower_factor = jnp.linalg.cholesky(gram_matrix)
    solved = lax.linalg.triangular_solve(lower_factor, lowpassed_record, left_side=True, lower=True)
    basis = solved.reshape(solved.shape[0], 1, solved.shape[1])
    return (lower_factor, basis)


def solution(mesh):
    placed = (P("tm", "space"), P())
    return jax.shard_map(
        per_device,
        mesh=mesh,
        in_specs=placed,
        out_specs=(P(), P(None, "space", "tm")),
        check_vma=False,
    )
```

profile of v0, /device:TPU:1, one launch (start us, length us, event | category | flops | bytes accessed | tf_op | source)
XLA Modules:
  0.0 528.4 jit_solution(12183669354091863755)
XLA Ops:
  7.2 0.0 all-reduce.3.cloned.1.call-start
  7.2 1.6 fusion.91
  8.8 5.4 %collective-permute-start = (f32[15,12288]{1,0:T(8,128)S(1)}, f32[15,12288]{1,0:T(8,128)S(1)}, u32[]{:S(2)}, u32[]{:S(2)}) collective-permute-start(f32[15,12288]{1,0:T(8,128)S(1)} %get-tuple-element.35), channel_id=1, source_target_pairs={{0,32},{32,64},{64,96},{96,128},{128,160},{160,192},{192,224},{224... | collective-permute-start | bytes 2211848 | tf_op jit(solution)/shard_map/ppermute | solution.py:14
  14.2 0.0 copy-start.5
  14.2 4.7 collective-permute-start.1
  19.0 0.1 constant_dynamic-update-slice_fusion.1
  19.1 0.7 fusion.93
  19.8 0.7 fusion.92
  20.5 7.0 %collective-permute-done.1 = f32[15,12288]{1,0:T(8,128)S(1)} collective-permute-done((f32[15,12288]{1,0:T(8,128)S(1)}, f32[15,12288]{1,0:T(8,128)S(1)}, u32[]{:S(2)}, u32[]{:S(2)}) %collective-permute-start.1) | collective-permute-done | bytes 737312 | tf_op jit(solution)/shard_map/ppermute | solution.py:15
  27.5 0.1 constant_dynamic-update-slice_fusion
  27.6 0.0 collective-permute-done
  27.6 26.0 %fusion.19 = f32[32,12288]{1,0:T(8,128)S(1)} fusion(f32[32,12288]{1,0:T(8,128)S(1)} %copy-done, f32[15,12288]{1,0:T(8,128)S(1)} %collective-permute-done, f32[47,12288]{1,0:T(8,128)S(1)} %constant_dynamic-update-slice_fusion, f32[]{:T(128)} %bitcast.30, f32[]{:T(128)} %bitcast.29, f32[]{:T(128)} %bitcast.28, f32[]{:T(128)} %bitcast.27, f32[]{:T(128)} %bitcast.26, ...), kind=kLoop, calls=%fused_computation.49 | loop fusion | flops 29884416 | bytes 27476092 | tf_op jit(solution)/shard_map/add | solution.py:24
  53.6 0.2 copy.25
  53.8 49.4 %all_to_all.19 = f32[32,16,768]{2,0,1:T(8,128)S(1)} all-to-all(f32[32,16,768]{2,0,1:T(8,128)S(1)} %bitcast.97), channel_id=1, replica_groups=mesh['tm'=16,'space'=32] {'tm'}, dimensions={1} | all-to-all | bytes 3145728 | tf_op jit(solution)/shard_map/all_to_all | solution.py:30
  103.2 3.7 fusion.94
  106.8 0.0 all-reduce.3.cloned.1.call-update
  106.9 1.1 fusion.90
  108.0 268.2 %all-reduce.3.cloned.1.call-done = f32[512,512]{0,1:T(8,128)} async-done(((f32[512,512]{0,1:T(8,128)}), f32[512,512]{0,1:T(8,128)}) %all-reduce.3.cloned.1.call-update) | async-done | bytes 1048592 | tf_op jit(solution)/shard_map/psum | solution.py:48
  376.1 1.3 broadcast_multiply_fusion
  377.5 0.3 copy.20
  377.8 0.9 copy-done.1
  378.7 0.2 fusion.64
  379.0 11.7 %cholesky.104 = f32[128,128]{1,0:T(8,128)S(1)} custom-call(f32[128,128]{1,0:T(8,128)S(1)} %cholesky.266), custom_call_target="Cholesky" | custom-call | tf_op jit(solution)/shard_map/jit(cholesky)/cholesky | solution.py:51
  390.7 0.1 cholesky.224
  390.8 9.8 %custom-call.30 = f32[1,128,128]{1,2,0:T(8,128)S(1)} custom-call(f32[1,128,128]{2,1,0:T(8,128)S(1)} %get-tuple-element.45), custom_call_target="InvertDiagBlocksLowerTriangular" | custom-call | tf_op jit(solution)/shard_map/jit(cholesky)/cholesky | solution.py:51
  400.6 0.3 constant_dynamic-update-slice_fusion.5
  401.0 0.3 convolution_subtract_fusion.3
  401.3 11.9 %cholesky.217 = f32[128,128]{1,0:T(8,128)S(1)} custom-call(f32[128,128]{1,0:T(8,128)S(1)} %cholesky.270), custom_call_target="Cholesky" | custom-call | tf_op jit(solution)/shard_map/jit(cholesky)/cholesky | solution.py:51
  413.2 9.8 %custom-call.31 = f32[1,128,128]{1,2,0:T(8,128)S(1)} custom-call(f32[1,128,128]{2,1,0:T(8,128)S(1)} %get-tuple-element.42), custom_call_target="InvertDiagBlocksLowerTriangular" | custom-call | tf_op jit(solution)/shard_map/jit(cholesky)/cholesky | solution.py:51
  423.0 0.3 convolution_dynamic-update-slice_fusion
  423.3 0.4 convolution_subtract_fusion.4
  423.7 11.7 %cholesky.238 = f32[128,128]{1,0:T(8,128)S(1)} custom-call(f32[128,128]{1,0:T(8,128)S(1)} %cholesky.275), custom_call_target="Cholesky" | custom-call | tf_op jit(solution)/shard_map/jit(cholesky)/cholesky | solution.py:51
  435.5 9.8 %custom-call.32 = f32[1,128,128]{1,2,0:T(8,128)S(1)} custom-call(f32[1,128,128]{2,1,0:T(8,128)S(1)} %get-tuple-element.39), custom_call_target="InvertDiagBlocksLowerTriangular" | custom-call | tf_op jit(solution)/shard_map/jit(cholesky)/cholesky | solution.py:51
  445.3 0.2 convolution_dynamic-update-slice_fusion.1
  445.5 0.4 convolution_subtract_fusion.5
  445.9 11.9 %cholesky.255 = f32[128,128]{1,0:T(8,128)S(1)} custom-call(f32[128,128]{1,0:T(8,128)S(1)} %convolution_subtract_fusion.5), custom_call_target="Cholesky" | custom-call | tf_op jit(solution)/shard_map/jit(cholesky)/cholesky | solution.py:51
  457.8 0.7 compare_reduce_fusion.1
  458.5 0.6 compare_reduce_fusion
  459.2 0.7 compare_reduce_fusion.2
  462.4 0.0 copy-start.2
  462.4 1.2 fusion.65
  463.6 10.5 %while.1 = (s32[]{:T(128)}, f32[512,512]{1,0:T(8,128)S(1)}, s32[4,2]{0,1:T(2,128)S(1)}, f32[4,128,128]{2,1,0:T(8,128)}, s32[]{:T(128)}) while((s32[]{:T(128)}, f32[512,512]{1,0:T(8,128)S(1)}, s32[4,2]{0,1:T(2,128)S(1)}, f32[4,128,128]{2,1,0:T(8,128)}, s32[]{:T(128)}) %tuple.69), condition=%wide.while_cond, body=%wide.while_body.sunk | while | flops 2 | bytes 132205 | solution.py:52
  463.6 0.1 constant_dynamic-slice_fusion.2
  463.7 0.6 fusion.104
  464.3 2.0 bitcast_dynamic-update-slice_fusion.2
  466.3 0.1 constant_dynamic-slice_fusion.2
  466.3 0.6 fusion.104
  466.9 2.0 bitcast_dynamic-update-slice_fusion.2
  468.9 0.1 constant_dynamic-slice_fusion.2
  469.0 0.6 fusion.104
  469.6 2.0 bitcast_dynamic-update-slice_fusion.2
  471.5 0.1 constant_dynamic-slice_fusion.2
  471.6 0.6 fusion.104
  472.2 2.0 bitcast_dynamic-update-slice_fusion.2
  474.2 40.2 %custom-call.33 = f32[4,128,128]{1,2,0:T(8,128)S(1)} custom-call(f32[4,128,128]{2,1,0:T(8,128)} %get-tuple-element.9), custom_call_target="InvertDiagBlocksLowerTriangular" | custom-call | tf_op jit(solution)/shard_map/triangular_solve | solution.py:52
  514.4 0.5 fusion.81
  514.9 0.5 convolution_subtract_fusion.1
  515.4 0.5 fusion.80
  515.9 0.6 convolution_subtract_fusion.2
  516.5 0.5 fusion.78
  517.0 0.9 convolution_subtract_fusion
  517.9 0.5 fusion.77
  518.5 0.1 maximum_bitcast_fusion
  518.6 2.8 copy.21
  (19 shorter events, 0.2 us)
Async XLA Ops:
  7.2 11.8 %copy-start = (f32[32,12288]{1,0:T(8,128)S(1)}, f32[32,12288]{1,0:T(8,128)}, u32[]{:S(2)}) copy-start(f32[32,12288]{1,0:T(8,128)} %param.2) | copy-start | bytes 4718596
  7.2 369.0 %all-reduce.3.cloned.1.call-start = ((), (), s32[]{:S(2)}) async-start(), calls=%async_computation.1 | async-start | bytes 2097152 | tf_op jit(solution)/shard_map/psum | solution.py:48
  8.8 18.8 %collective-permute-start = (f32[15,12288]{1,0:T(8,128)S(1)}, f32[15,12288]{1,0:T(8,128)S(1)}, u32[]{:S(2)}, u32[]{:S(2)}) collective-permute-start(f32[15,12288]{1,0:T(8,128)S(1)} %get-tuple-element.35), channel_id=1, source_target_pairs={{0,32},{32,64},{64,96},{96,128},{128,160},{160,192},{192,224},{224... | collective-permute-start | bytes 2211848 | tf_op jit(solution)/shard_map/ppermute | solution.py:14
  14.2 4.9 copy-start.5
  14.2 13.3 %collective-permute-start.1 = (f32[15,12288]{1,0:T(8,128)S(1)}, f32[15,12288]{1,0:T(8,128)S(1)}, u32[]{:S(2)}, u32[]{:S(2)}) collective-permute-start(f32[15,12288]{1,0:T(8,128)S(1)} %get-tuple-element.34), channel_id=1, source_target_pairs={{32,0},{64,32},{96,64},{128,96},{160,128},{192,160},{224,192},{256... | collective-permute-start | bytes 2211848 | tf_op jit(solution)/shard_map/ppermute | solution.py:15
  377.5 1.2 copy-start.1
  462.4 52.0 %copy-start.2 = (f32[4,32,768]{2,1,0:T(8,128)S(1)}, f32[4,32,768]{2,1,0:T(8,128)}, u32[]{:S(2)}) copy-start(f32[4,32,768]{2,1,0:T(8,128)} %get-tuple-element.30) | copy-start | bytes 1179652
  474.2 41.7 %copy-start.4 = (f32[4,32,768]{2,1,0:T(8,128)S(1)}, f32[4,32,768]{2,1,0:T(8,128)}, u32[]{:S(2)}) copy-start(f32[4,32,768]{2,1,0:T(8,128)} %get-tuple-element.31) | copy-start | bytes 1179652
  515.4 1.7 copy-start.3
Sparse Core Ops, SparseCore 0:
  107.0 269.0 all-reduce.2
where the time goes:
time: 532 us; the launch traced here: 528 us
  waiting for transfers between devices  275 us (52%)
  other arithmetic  148 us (28%)
  blocking collectives  49.4 us (9%)
  local copies, waits for them, and re-layouts  19.1 us (4%)
  between operations  17.1 us (3%)
  starting transfers between devices  10.2 us (2%)
  matrix products  9.54 us (2%)
    psum x1, waiting for transfers between devices, per_device(): gram_matrix = lax.psum(local_gram, ('tm', 'space'))  268 us
    another operation x14, other arithmetic, per_device(): lower_factor = jnp.linalg.cholesky(gram_matrix)  78.8 us
    all_to_all x1, blocking collectives, resample_grid_points(): return lax.all_to_all(slab, 'tm', split_axis=1, concat_axis=0, tiled=True)  49.4 us
    another operation x3, other arithmetic, per_device(): lax.linalg.triangular_solve(lower_factor, lowpassed_record, left_side=Tru...  41.4 us
    add x1, other arithmetic, apply_filter_weights(): summed + filter_weights[offset] * boundary_extended_record[offset:offset...  26 us
  transfers between devices with their start and end apart: 3, of which 2 were waited for; matrix products, arithmetic and copies ran while one was open for 1% of the time, Pallas kernels for 0%

commit v1 on v0

v1 whole, which is shorter than its diff:
```python
import functools
import jax
import jax.numpy as jnp
from jax import lax
from jax.experimental import pallas as pl
from jax.experimental.pallas import tpu as pltpu
from jax.sharding import PartitionSpec as P

MESH = pl.DeviceIdType.MESH
ALONG_X = 4
B = 128
OFF = (0, 4, 7, 9)
HI = lax.Precision.HIGHEST


def dot(a, b, dims=((1,), (0,))):
    return lax.dot_general(a, b, (dims, ((), ())), precision=HI, preferred_element_type=jnp.float32)


def recip(d):
    r = pl.reciprocal(d, approx=True)
    return r * (2.0 - d * r)


def rsq(d):
    r = lax.rsqrt(d)
    return r * (1.5 - 0.5 * d * r * r)


def factor128(rows):
    n = len(rows)
    lane = lax.broadcasted_iota(jnp.int32, (8, B), 1)
    sub = lax.broadcasted_iota(jnp.int32, (8, B), 0)
    m = list(rows)
    upper, inverse = [], []
    for v in range(n):
        j = 8 * v
        g = m[v]
        col = [jnp.broadcast_to(g[:, j + k : j + k + 1], (8, B)) for k in range(8)]
        p = {}
        for k in range(8):
            for l in range(k, 8):
                p[l, k] = jnp.broadcast_to(col[k][l : l + 1, :], (8, B))
        ra = [jnp.broadcast_to(g[l : l + 1, :], (8, B)) for l in range(8)]
        inside = (lane >= j) & (lane < j + 8)
        ri = [jnp.where(inside, jnp.where(lane == j + l, 1.0, 0.0), ra[l]) for l in range(8)]
        inv, mult = [], {}
        for k in range(8):
            inv.append(recip(p[k, k]))
            for l in range(k + 1, 8):
                mult[l, k] = p[l, k] * inv[k]
            for c in range(k + 1, 8):
                for l in range(c, 8):
                    p[l, c] = p[l, c] - mult[l, k] * p[c, k]
            for l in range(k + 1, 8):
                ra[l] = ra[l] - mult[l, k] * ra[k]
                ri[l] = ri[l] - mult[l, k] * ri[k]
        q = [None] * 8
        for l in range(7, -1, -1):
            t = ri[l] * inv[l]
            for r in range(7, l, -1):
                t = t - mult[r, l] * q[r]
            q[l] = t
        for i in range(v + 1, n):
            ci = [jnp.broadcast_to(m[i][:, j + k : j + k + 1], (8, B)) for k in range(8)]
            t = jnp.where(inside, 0.0, m[i])
            s1 = ci[0] * q[0] + ci[1] * q[1]
            s2 = ci[2] * q[2] + ci[3] * q[3]
            s3 = ci[4] * q[4] + ci[5] * q[5]
            s4 = ci[6] * q[6] + ci[7] * q[7]
            m[i] = t - ((s1 + s2) + (s3 + s4))
        u = jnp.zeros((8, B), jnp.float32)
        w = u
        for l in range(8):
            r = rsq(p[l, l])
            u = jnp.where(sub == l, ra[l] * r, u)
            w = jnp.where(sub == l, ri[l] * r, w)
        upper.append(jnp.where(lane >= j + sub, u, 0.0))
        inverse.append(jnp.where(lane <= j + sub, w, 0.0))
    return upper, inverse


def body(scale, g_ref, fx_ref, l_ref, y_ref, a, u, t, f):
    f[...] = fx_ref[...]
    for b in range(10):
        a[b] = g_ref[pl.ds(b * B, B), :] * scale
    l_ref[...] = jnp.zeros_like(l_ref)
    for k in range(4):
        d = OFF[k]
        rows = [a[d, pl.ds(8 * v, 8), :] for v in range(16)]
        up, iv = factor128(rows)
        for v in range(16):
            u[pl.ds(8 * v, 8), :] = up[v]
            t[pl.ds(8 * v, 8), :] = iv[v]
        tk = t[...]
        l_ref[pl.ds(k * B, B), pl.ds(k * B, B)] = u[...].T
        low = {}
        for i in range(k + 1, 4):
            low[i] = dot(a[d + i - k], tk, ((1,), (1,)))
            l_ref[pl.ds(i * B, B), pl.ds(k * B, B)] = low[i]
        for j in range(k + 1, 4):
            for i in range(j, 4):
                e = OFF[j] + i - j
                a[e] = a[e] - dot(low[i], low[j], ((1,), (1,)))
        y = dot(tk, f[pl.ds(k * B, B), :])
        for i in range(k + 1, 4):
            f[pl.ds(i * B, B), :] = f[pl.ds(i * B, B), :] - dot(low[i], y)
        wide = f.shape[1] // B
        for q in range(wide):
            y_ref[pl.ds(k * B * wide + q, B, stride=wide), :] = y[:, q * B : (q + 1) * B]


def factor_and_solve(gram, fx, points):
    rows, cols = fx.shape
    return pl.pallas_call(
        functools.partial(body, 1.0 / points),
        out_shape=(
            jax.ShapeDtypeStruct((rows, rows), jnp.float32),
            jax.ShapeDtypeStruct((rows * cols // B, B), jnp.float32),
        ),
        in_specs=[pl.BlockSpec(memory_space=pltpu.VMEM)] * 2,
        out_specs=(pl.BlockSpec(memory_space=pltpu.VMEM),) * 2,
        scratch_shapes=[
            pltpu.VMEM((10, B, B), jnp.float32),
            pltpu.VMEM((B, B), jnp.float32),
            pltpu.VMEM((B, B), jnp.float32),
            pltpu.VMEM((rows, cols), jnp.float32),
        ],
        compiler_params=pltpu.CompilerParams(vmem_limit_bytes=48 << 20),
        name="factor",
    )(gram, fx)


BLOCK = 128
CHUNK = 256
ORDER = ((0, 0), (1, 0), (2, 0), (3, 0), (1, 1), (2, 1), (3, 1), (2, 2), (3, 2), (3, 3))


class Plan:
    def __init__(self, mesh, nx, rows, width, taps):
        self.tm, self.space = mesh.shape["tm"], mesh.shape["space"]
        self.nz, self.nx, self.ny = self.tm // 2, nx, self.space // nx
        self.rows, self.width, self.taps = rows, width, taps
        self.time = rows * self.tm
        self.chunks = width // CHUNK
        self.packed = len(ORDER) * BLOCK
        self.half = self.packed // 2
        self.part = self.half // self.nx
        self.piece = -(-self.part // (8 * self.ny)) * 8
        self.padded = self.piece * self.ny


def remote(src, dst, send, recv, where):
    return pltpu.make_async_remote_copy(
        src_ref=src, dst_ref=dst, send_sem=send, recv_sem=recv, device_id=where, device_id_type=MESH
    )


def gather_body(plan, w_ref, x_ref, fx_ref, g_ref, xr, band, acc, p, rc, rx, hx, ry, hy, rz, gy, o,
                xs, xd, xl, cs, cd, ss, sd, ys, yd, zs, zd, yas, yad, xas, xad, cas, cad):
    P = plan
    t, s = lax.axis_index("tm"), lax.axis_index("space")
    z, c = t // 2, t % 2
    y, x = s // P.nx, s % P.nx

    def at_tm(i):
        return {"tm": i}

    def at_x(d):
        return {"space": y * P.nx + (x + d) % P.nx}

    def at_y(d):
        return {"space": ((y + d) % P.ny) * P.nx + x}

    def at_z(d):
        return {"tm": ((z + d) % P.nz) * 2 + c}

    sibling = {"tm": z * 2 + (1 - c)}

    barrier = pltpu.get_barrier_semaphore()
    for d in range(1, P.tm):
        pl.semaphore_signal(barrier, inc=1, device_id=at_tm((t + d) % P.tm), device_id_type=MESH)
    for d in range(1, P.nx):
        pl.semaphore_signal(barrier, inc=1, device_id=at_x(d), device_id_type=MESH)
    for d in range(1, P.ny):
        pl.semaphore_signal(barrier, inc=1, device_id=at_y(d), device_id_type=MESH)
    pl.semaphore_wait(barrier, (P.tm - 1) + (P.nx - 1) + (P.ny - 1))

    mine = pl.ds(pl.multiple_of(t * P.rows, 8), P.rows)
    steps = sorted(range(1, P.tm), key=lambda d: -min(d, P.tm - d))
    sends, local = [], []
    for h in range(P.chunks):
        there = pl.ds(h * CHUNK, CHUNK)
        for d in steps:
            peer = (t + d) % P.tm
            src = x_ref.at[:, pl.ds(pl.multiple_of(peer * P.width + h * CHUNK, 128), CHUNK)]
            copy = remote(src, xr.at[mine, there], xs.at[h, d - 1], xd.at[h], at_tm(peer))
            copy.start()
            sends.append(copy)
        own = pltpu.make_async_copy(
            x_ref.at[:, pl.ds(pl.multiple_of(t * P.width + h * CHUNK, 128), CHUNK)],
            xr.at[mine, there], xl.at[h])
        own.start()
        local.append(own)

    r = lax.broadcasted_iota(jnp.int32, (BLOCK, 3 * BLOCK), 0)
    q = lax.broadcasted_iota(jnp.int32, (BLOCK, 3 * BLOCK), 1)
    tap = q - r - BLOCK + (P.taps - 1) // 2
    f = jnp.zeros((BLOCK, 3 * BLOCK), jnp.float32)
    for k in range(P.taps):
        f = jnp.where(tap == k, w_ref[k], f)
    band[...] = f

    nb = P.time // BLOCK
    for h in range(P.chunks):
        there = pl.ds(h * CHUNK, CHUNK)
        local[h].wait()
        rest = xr.at[pl.ds(0, P.time - P.rows), there]
        pltpu.make_async_copy(rest, rest, xd.at[h]).wait()
        for i in range(nb):
            lo, hi = max(i - 1, 0), min(i + 2, nb)
            fx_ref[pl.ds(i * BLOCK, BLOCK), there] = dot(
                band[:, (lo - i + 1) * BLOCK : (hi - i + 1) * BLOCK],
                xr[pl.ds(lo * BLOCK, (hi - lo) * BLOCK), there])
        top = fx_ref[pl.ds(0, 256), there]
        low = fx_ref[pl.ds(256, 256), there]
        for e, (u, v) in enumerate(((top, top), (low, top), (low, low))):
            new = dot(u, v, ((1,), (1,)))
            if h > 0:
                new = acc[e] + new
            if h < P.chunks - 1:
                acc[e] = new
            else:
                for b, (i, j) in enumerate(ORDER):
                    if ((0, 0), (1, 0), (1, 1))[e] == (i // 2, j // 2):
                        p[pl.ds(b * BLOCK, BLOCK), :] = new[
                            (i % 2) * BLOCK : (i % 2 + 1) * BLOCK, (j % 2) * BLOCK : (j % 2 + 1) * BLOCK]

    def half(i):
        return pl.ds(pl.multiple_of(i * P.half, 8), P.half)

    copy = remote(p.at[half(1 - c)], rc, cs, cd, sibling)
    copy.start()
    for done in sends:
        done.wait_send()
    copy.wait()
    p[half(c), :] = p[half(c), :] + rc[...]

    def part(i):
        return pl.ds(pl.multiple_of((c * P.nx + i) * P.part, 8), P.part)

    copies = [remote(p.at[part((x + d) % P.nx)], rx.at[d - 1], ss.at[d - 1], sd.at[d - 1], at_x(d))
              for d in range(1, P.nx)]
    for copy in copies:
        copy.start()
    if P.padded > P.part:
        hx[pl.ds(P.part, P.padded - P.part), :] = jnp.zeros((P.padded - P.part, BLOCK), jnp.float32)
    total = p[part(x), :]
    for d, copy in enumerate(copies):
        copy.wait()
        total = total + rx[d]
    hx[pl.ds(0, P.part), :] = total

    def piece(i):
        return pl.ds(pl.multiple_of(i * P.piece, 8), P.piece)

    copies = [remote(hx.at[piece((y + d) % P.ny)], ry.at[d - 1], ys.at[d - 1], yd.at[d - 1], at_y(d))
              for d in range(1, P.ny)]
    for copy in copies:
        copy.start()
    total = hx[piece(y), :]
    for d, copy in enumerate(copies):
        copy.wait()
        total = total + ry[d]
    hy[...] = total

    copies = [remote(hy, rz.at[z], zs.at[d - 1], zd.at[d - 1], at_z(d)) for d in range(1, P.nz)]
    for copy in copies:
        copy.start()
    rz[z] = total
    for copy in copies:
        copy.wait()
    total = rz[0]
    for i in range(1, P.nz):
        total = total + rz[i]
    gy[piece(y), :] = total

    copies = [remote(gy.at[piece(y)], gy.at[piece(y)], yas.at[d - 1], yad.at[d - 1], at_y(d))
              for d in range(1, P.ny)]
    for copy in copies:
        copy.start()
    for copy in copies:
        copy.wait()
    copies = [remote(gy.at[pl.ds(0, P.part)], o.at[part(x)], xas.at[d - 1], xad.at[d - 1], at_x(d))
              for d in range(1, P.nx)]
    for copy in copies:
        copy.start()
    o[part(x), :] = gy[pl.ds(0, P.part), :]
    for copy in copies:
        copy.wait()
    copy = remote(o.at[half(c)], o.at[half(c)], cas, cad, sibling)
    copy.start()
    copy.wait()
    g_ref[...] = o[...]


def filter_and_gram(plan, weights, record):
    P = plan
    f32, dma = jnp.float32, pltpu.SemaphoreType.DMA
    x, y, z = P.nx - 1, P.ny - 1, P.nz - 1
    return pl.pallas_call(
        functools.partial(gather_body, plan),
        out_shape=(
            jax.ShapeDtypeStruct((P.time, P.width), f32),
            jax.ShapeDtypeStruct((P.packed, BLOCK), f32),
        ),
        in_specs=[pl.BlockSpec(memory_space=pltpu.SMEM), pl.BlockSpec(memory_space=pl.ANY)],
        out_specs=(pl.BlockSpec(memory_space=pltpu.VMEM),) * 2,
        scratch_shapes=[
            pltpu.VMEM((P.time, P.width), f32),
            pltpu.VMEM((BLOCK, 3 * BLOCK), f32),
            pltpu.VMEM((3, 256, 256), f32),
            pltpu.VMEM((P.packed, BLOCK), f32),
            pltpu.VMEM((P.half, BLOCK), f32),
            pltpu.VMEM((x, P.part, BLOCK), f32),
            pltpu.VMEM((P.padded, BLOCK), f32),
            pltpu.VMEM((y, P.piece, BLOCK), f32),
            pltpu.VMEM((P.piece, BLOCK), f32),
            pltpu.VMEM((P.nz, P.piece, BLOCK), f32),
            pltpu.VMEM((P.padded, BLOCK), f32),
            pltpu.VMEM((P.packed, BLOCK), f32),
            dma((P.chunks, P.tm - 1)), dma((P.chunks,)), dma((P.chunks,)),
            dma, dma, dma((x,)), dma((x,)), dma((y,)), dma((y,)), dma((z,)), dma((z,)),
            dma((y,)), dma((y,)), dma((x,)), dma((x,)), dma, dma,
        ],
        compiler_params=pltpu.CompilerParams(
            collective_id=0, has_side_effects=True, vmem_limit_bytes=48 << 20),
        name="gather_filter_gram",
    )(weights, record)


def solution(mesh):
    def per_device(record, weights):
        rows, width = record.shape[0], record.shape[1] // mesh.shape["tm"]
        plan = Plan(mesh, ALONG_X, rows, width, weights.shape[0])
        fx, gram = filter_and_gram(plan, weights, record)
        points = width * mesh.shape["tm"] * mesh.shape["space"]
        lower, basis = factor_and_solve(gram, fx, points)
        return lower, basis.reshape(plan.time, 1, width)

    return jax.shard_map(
        per_device,
        mesh=mesh,
        in_specs=(P("tm", "space"), P()),
        out_specs=(P(), P(None, "space", "tm")),
        check_vma=False,
    )
```

time: 532 us -> 114 us (0.21)
  waiting for transfers between devices: 275 us -> 0 us
  other arithmetic: 148 us -> 0 us
  Pallas kernels: 0 us -> 112 us
  blocking collectives: 49.4 us -> 0 us
  local copies, waits for them, and re-layouts: 19.1 us -> 2.06 us
  between operations: 17.1 us -> 0.65 us
  starting transfers between devices: 10.2 us -> 0 us
  matrix products: 9.54 us -> 0 us
    psum x1 -> x0, waiting for transfers between devices: 268 us -> none  [per_device(): gram_matrix = lax.psum(local_gram, ('tm', 'space'))]
    another operation x17 -> x0, other arithmetic: 120 us -> none  [the longest x14 78.8 us: per_device(): lower_factor = jnp.linalg.cholesky(gram_matrix)]
    pallas_call x0 -> x2, Pallas kernels: none -> 112 us  [the longest x1 83.9 us: filter_and_gram(): pl.pallas_call(functools.partial(gather_body, plan), out_shape=(jax.Shape...]
    all_to_all x1 -> x0, blocking collectives: 49.4 us -> none  [resample_grid_points(): return lax.all_to_all(slab, 'tm', split_axis=1, concat_axis=0, tiled=True)]
    add x1 -> x0, other arithmetic: 26 us -> none  [apply_filter_weights(): summed + filter_weights[offset] * boundary_extended_record[offset:offset...]
    another operation x18 -> x0, local copies, waits for them, and re-layouts: 11.7 us -> none
    ppermute x2 -> x0, starting transfers between devices: 10.1 us -> none  [the longest x1 5.39 us: padded(): before = lax.ppermute(last, axis, up)]
    ppermute x2 -> x0, waiting for transfers between devices: 7 us -> none  [the longest x1 7 us: padded(): after = lax.ppermute(initial, axis, down)]
  transfers between devices with their start and end apart: 3 -> 0, of which waited for: 2 -> 0; matrix products, arithmetic and copies ran while one was open for 1% -> 0% of each run, Pallas kernels for 0% -> 0%
where the time goes in v1:
time: 114 us
  Pallas kernels  112 us (98%)
  local copies, waits for them, and re-layouts  2.06 us (2%)
    pallas_call x1, Pallas kernels, filter_and_gram(): pl.pallas_call(functools.partial(gather_body, plan), out_shape=(jax.Shape...  83.9 us
    pallas_call x1, Pallas kernels, factor_and_solve(): pl.pallas_call(functools.partial(body, 1.0 / points), out_shape=(jax.Shap...  27.7 us

profile of v1, /device:TPU:1, one launch (start us, length us, event | category | flops | bytes accessed | tf_op | source)
XLA Modules:
  0.0 114.3 jit_solution(13539111805439362817)
XLA Ops:
  0.6 0.0 copy-start
  0.6 1.4 %copy-done = f32[32,12288]{1,0:T(8,128)S(1)} copy-done((f32[32,12288]{1,0:T(8,128)S(1)}, f32[32,12288]{1,0:T(8,128)}, u32[]{:S(2)}) %copy-start) | copy-done | bytes 1572888
  2.0 0.0 copy-start.1
  2.0 0.7 copy-done.1
  2.7 83.9 %gather_filter_gram.1 = (f32[512,768]{1,0:T(8,128)S(1)}, f32[1280,128]{1,0:T(8,128)S(1)}) custom-call(f32[31]{0:T(128)S(1)} %copy-done.1, f32[32,12288]{1,0:T(8,128)S(1)} %copy-done), custom_call_target="tpu_custom_call" | custom-call | tf_op jit(solution)/shard_map/gather_filter_gram/pallas_call | solution.py:311
  86.6 27.7 %factor.1 = (f32[512,512]{1,0:T(8,128)}, f32[3072,128]{1,0:T(8,128)}) custom-call(f32[1280,128]{1,0:T(8,128)S(1)} %get-tuple-element.6.g_ref, f32[512,768]{1,0:T(8,128)S(1)} %get-tuple-element.7.fx_ref), custom_call_target="tpu_custom_call" | custom-call | tf_op jit(solution)/shard_map/factor/pallas_call | solution.py:115
Async XLA Ops:
  0.6 1.4 %copy-start = (f32[32,12288]{1,0:T(8,128)S(1)}, f32[32,12288]{1,0:T(8,128)}, u32[]{:S(2)}) copy-start(f32[32,12288]{1,0:T(8,128)} %x_ref.1) | copy-start | bytes 4718596
  2.0 0.7 copy-start.1

commit v2 on v1

v2 whole, which is shorter than its diff:
```python
import functools
import jax
import jax.numpy as jnp
from jax import lax
from jax.experimental import pallas as pl
from jax.experimental.pallas import tpu as pltpu
from jax.sharding import PartitionSpec as P

MESH = pl.DeviceIdType.MESH
ALONG_X = 4
B = 128
OFF = (0, 4, 7, 9)
HI = lax.Precision.HIGHEST


def dot(a, b, dims=((1,), (0,))):
    return lax.dot_general(a, b, (dims, ((), ())), precision=HI, preferred_element_type=jnp.float32)


def recip(d):
    return pl.reciprocal(d, approx=True)


def rsq(d):
    r = lax.rsqrt(d)
    return r


def factor128(rows, cs, gs):
    n = len(rows)
    lane = lax.broadcasted_iota(jnp.int32, (8, B), 1)
    sub = lax.broadcasted_iota(jnp.int32, (8, B), 0)
    m = list(rows)
    upper, inverse = [], []
    for v in range(n):
        j = 8 * v
        g = m[v]
        col = [jnp.broadcast_to(g[:, j + k : j + k + 1], (8, B)) for k in range(8)]
        p = {}
        o = v % 2
        gs[o] = g
        for k in range(8):
            cs[o, k] = col[k]
        for k in range(8):
            for l in range(k, 8):
                p[l, k] = jnp.broadcast_to(cs[o, k, pl.ds(l, 1), :], (8, B))
        ra = [jnp.broadcast_to(gs[o, pl.ds(l, 1), :], (8, B)) for l in range(8)]
        inside = (lane >= j) & (lane < j + 8)
        ri = [jnp.where(inside, jnp.where(lane == j + l, 1.0, 0.0), ra[l]) for l in range(8)]
        piv, n0, n1 = [None] * 8, {}, {}
        qa = [None] * 8
        for k in range(0, 8, 2):
            e = k + 1
            det = p[k, k] * p[e, e] - p[e, k] * p[e, k]
            rd = recip(det)
            i00, i10, i11 = p[e, e] * rd, -p[e, k] * rd, p[k, k] * rd
            for l in range(k + 2, 8):
                n0[l, k] = p[l, k] * i00 + p[l, e] * i10
                n1[l, k] = p[l, k] * i10 + p[l, e] * i11
            for c in range(k + 2, 8):
                for l in range(c, 8):
                    p[l, c] = p[l, c] - (n0[l, k] * p[c, k] + n1[l, k] * p[c, e])
            for l in range(k + 2, 8):
                ra[l] = ra[l] - (n0[l, k] * ra[k] + n1[l, k] * ra[e])
                ri[l] = ri[l] - (n0[l, k] * ri[k] + n1[l, k] * ri[e])
            qa[k] = i00 * ri[k] + i10 * ri[e]
            qa[e] = i10 * ri[k] + i11 * ri[e]
            first = recip(p[k, k])
            mult = p[e, k] * first
            ra[e] = ra[e] - mult * ra[k]
            ri[e] = ri[e] - mult * ri[k]
            p[e, e] = det * first
        q = list(qa)
        for k in (4, 2, 0):
            for l in range(7, k + 1, -1):
                q[k] = q[k] - n0[l, k] * q[l]
                q[k + 1] = q[k + 1] - n1[l, k] * q[l]
        for i in range(v + 1, n):
            ci = [jnp.broadcast_to(m[i][:, j + k : j + k + 1], (8, B)) for k in range(8)]
            t = jnp.where(inside, 0.0, m[i])
            s1 = ci[0] * q[0] + ci[1] * q[1]
            s2 = ci[2] * q[2] + ci[3] * q[3]
            s3 = ci[4] * q[4] + ci[5] * q[5]
            s4 = ci[6] * q[6] + ci[7] * q[7]
            m[i] = t - ((s1 + s2) + (s3 + s4))
        u = jnp.zeros((8, B), jnp.float32)
        w = u
        for l in range(8):
            r = rsq(p[l, l])
            u = jnp.where(sub == l, ra[l] * r, u)
            w = jnp.where(sub == l, ri[l] * r, w)
        upper.append(jnp.where(lane >= j + sub, u, 0.0))
        inverse.append(jnp.where(lane <= j + sub, w, 0.0))
    return upper, inverse


def body(scale, g_ref, fx_ref, l_ref, y_ref, a, u, t, f, cs, gs):
    eye = lax.broadcasted_iota(jnp.int32, (B, B), 0) == lax.broadcasted_iota(jnp.int32, (B, B), 1)
    across, down, root = [], [], []
    for k in range(4):
        kept = jnp.where(eye, g_ref[pl.ds(OFF[k] * B, B), :] * scale, 0.0)
        across.append(rsq(jnp.sum(kept, axis=0, keepdims=True)))
        column = jnp.sum(kept, axis=1, keepdims=True)
        down.append(rsq(column))
        root.append(column * down[k])
    for k in range(4):
        for i in range(k, 4):
            b = OFF[k] + i - k
            a[b] = (g_ref[pl.ds(b * B, B), :] * scale) * down[i] * across[k]
        f[pl.ds(k * B, B), :] = fx_ref[pl.ds(k * B, B), :] * down[k]
    l_ref[...] = jnp.zeros_like(l_ref)
    for k in range(4):
        d = OFF[k]
        rows = [a[d, pl.ds(8 * v, 8), :] for v in range(16)]
        up, iv = factor128(rows, cs, gs)
        for v in range(16):
            u[pl.ds(8 * v, 8), :] = up[v]
            t[pl.ds(8 * v, 8), :] = iv[v]
        tk = t[...]
        l_ref[pl.ds(k * B, B), pl.ds(k * B, B)] = u[...].T * root[k]
        low = {}
        for i in range(k + 1, 4):
            low[i] = dot(a[d + i - k], tk, ((1,), (1,)))
            l_ref[pl.ds(i * B, B), pl.ds(k * B, B)] = low[i] * root[i]
            for j in range(k + 1, i + 1):
                e = OFF[j] + i - j
                a[e] = a[e] - dot(low[i], low[j], ((1,), (1,)))
        y = dot(tk, f[pl.ds(k * B, B), :])
        for i in range(k + 1, 4):
            f[pl.ds(i * B, B), :] = f[pl.ds(i * B, B), :] - dot(low[i], y)
        wide = f.shape[1] // B
        for q in range(wide):
            y_ref[pl.ds(k * B * wide + q, B, stride=wide), :] = y[:, q * B : (q + 1) * B]


def factor_and_solve(gram, fx, points):
    rows, cols = fx.shape
    return pl.pallas_call(
        functools.partial(body, 1.0 / points),
        out_shape=(
            jax.ShapeDtypeStruct((rows, rows), jnp.float32),
            jax.ShapeDtypeStruct((rows * cols // B, B), jnp.float32),
        ),
        in_specs=[pl.BlockSpec(memory_space=pltpu.VMEM)] * 2,
        out_specs=(pl.BlockSpec(memory_space=pltpu.VMEM),) * 2,
        scratch_shapes=[
            pltpu.VMEM((10, B, B), jnp.float32),
            pltpu.VMEM((B, B), jnp.float32),
            pltpu.VMEM((B, B), jnp.float32),
            pltpu.VMEM((rows, cols), jnp.float32),
            pltpu.VMEM((2, 8, 8, B), jnp.float32),
            pltpu.VMEM((2, 8, B), jnp.float32),
        ],
        compiler_params=pltpu.CompilerParams(vmem_limit_bytes=48 << 20),
        name="factor",
    )(gram, fx)


BLOCK = 128
CHUNK = 256
ORDER = ((0, 0), (1, 0), (2, 0), (3, 0), (1, 1), (2, 1), (3, 1), (2, 2), (3, 2), (3, 3))


class Stream:
    def __init__(self, first, count, plan):
        self.base, self.packed = first * BLOCK, count * BLOCK
        self.half = self.packed // 2
        self.part = self.half // plan.nx
        self.piece = -(-self.part // (8 * plan.ny)) * 8
        self.padded = self.piece * plan.ny

    def buffers(self, plan):
        x, y, z = plan.nx - 1, plan.ny - 1, plan.nz - 1
        shapes = [
            (self.packed, BLOCK), (self.half, BLOCK), (x, self.part, BLOCK), (self.padded, BLOCK),
            (y, self.piece, BLOCK), (self.piece, BLOCK), (plan.nz, self.piece, BLOCK),
            (self.padded, BLOCK), (self.packed, BLOCK)]
        dma = pltpu.SemaphoreType.DMA
        counts = [1, 1, x, x, y, y, z, z, y, y, x, x, 1, 1]
        return [pltpu.VMEM(shape, jnp.float32) for shape in shapes] + [dma((n,)) for n in counts]


class Plan:
    def __init__(self, mesh, nx, rows, width, taps):
        self.tm, self.space = mesh.shape["tm"], mesh.shape["space"]
        self.nz, self.nx, self.ny = self.tm // 2, nx, self.space // nx
        self.rows, self.width, self.taps = rows, width, taps
        self.time = rows * self.tm
        self.chunks = width // CHUNK
        self.streams = [Stream(first, count, self) for first, count in ((0, 4), (4, 6))]


def remote(src, dst, send, recv, where):
    return pltpu.make_async_remote_copy(
        src_ref=src, dst_ref=dst, send_sem=send, recv_sem=recv, device_id=where, device_id_type=MESH
    )


def gather_body(plan, w_hbm, x_ref, fx_ref, g_ref, w_ref, xr, band, acc, ws, xs, xd, xl, *rest):
    P = plan
    t, s = lax.axis_index("tm"), lax.axis_index("space")
    z, c = t // 2, t % 2
    y, x = s // P.nx, s % P.nx

    def at_tm(i):
        return {"tm": i}

    def at_x(d):
        return {"space": y * P.nx + (x + d) % P.nx}

    def at_y(d):
        return {"space": ((y + d) % P.ny) * P.nx + x}

    def at_z(d):
        return {"tm": ((z + d) % P.nz) * 2 + c}

    sibling = {"tm": z * 2 + (1 - c)}

    weights = pltpu.make_async_copy(w_hbm, w_ref, ws)
    weights.start()
    barrier = pltpu.get_barrier_semaphore()
    for d in range(1, P.tm):
        pl.semaphore_signal(barrier, inc=1, device_id=at_tm((t + d) % P.tm), device_id_type=MESH)
    for d in range(1, P.nx):
        pl.semaphore_signal(barrier, inc=1, device_id=at_x(d), device_id_type=MESH)
    for d in range(1, P.ny):
        pl.semaphore_signal(barrier, inc=1, device_id=at_y(d), device_id_type=MESH)
    pl.semaphore_wait(barrier, (P.tm - 1) + (P.nx - 1) + (P.ny - 1))

    mine = pl.ds(pl.multiple_of(t * P.rows, 8), P.rows)
    steps = sorted(range(1, P.tm), key=lambda d: -min(d, P.tm - d))
    sends, local = [], []
    for h in range(P.chunks):
        there = pl.ds(h * CHUNK, CHUNK)
        for d in steps:
            peer = (t + d) % P.tm
            src = x_ref.at[:, pl.ds(pl.multiple_of(peer * P.width + h * CHUNK, 128), CHUNK)]
            copy = remote(src, xr.at[mine, there], xs.at[h, d - 1], xd.at[h], at_tm(peer))
            copy.start()
            sends.append(copy)
        own = pltpu.make_async_copy(
            x_ref.at[:, pl.ds(pl.multiple_of(t * P.width + h * CHUNK, 128), CHUNK)],
            xr.at[mine, there], xl.at[h])
        own.start()
        local.append(own)

    r = lax.broadcasted_iota(jnp.int32, (BLOCK, 3 * BLOCK), 0)
    q = lax.broadcasted_iota(jnp.int32, (BLOCK, 3 * BLOCK), 1)
    weights.wait()
    tap = q - r - BLOCK + (P.taps - 1) // 2
    f = jnp.zeros((BLOCK, 3 * BLOCK), jnp.float32)
    for k in range(P.taps):
        f = jnp.where(tap == k, w_ref[k], f)
    band[...] = f

    size = len(rest) // len(P.streams)
    held = [rest[i * size : (i + 1) * size] for i in range(len(P.streams))]
    sums = [sum_everywhere(P, S, (at_x, at_y, at_z, sibling), (z, c, y, x), one)
            for S, one in zip(P.streams, held)]
    nb = P.time // BLOCK
    for h in range(P.chunks):
        there = pl.ds(h * CHUNK, CHUNK)
        local[h].wait()
        others = xr.at[pl.ds(0, P.time - P.rows), there]
        pltpu.make_async_copy(others, others, xd.at[h]).wait()
        for i in range(nb):
            lo, hi = max(i - 1, 0), min(i + 2, nb)
            fx_ref[pl.ds(i * BLOCK, BLOCK), there] = dot(
                band[:, (lo - i + 1) * BLOCK : (hi - i + 1) * BLOCK],
                xr[pl.ds(lo * BLOCK, (hi - lo) * BLOCK), there])
        top = fx_ref[pl.ds(0, 256), there]
        low = fx_ref[pl.ds(256, 256), there]
        for e, (u, v) in enumerate(((top, top), (low, top), (low, low))):
            new = dot(u, v, ((1,), (1,)))
            if h > 0:
                new = acc[e] + new
            if h < P.chunks - 1:
                acc[e] = new
                continue
            for n, (i, j) in enumerate(ORDER):
                if ((0, 0), (1, 0), (1, 1))[e] == (i // 2, j // 2):
                    st = 0 if n < 4 else 1
                    held[st][0][pl.ds(n * BLOCK - P.streams[st].base, BLOCK), :] = new[
                        (i % 2) * BLOCK : (i % 2 + 1) * BLOCK, (j % 2) * BLOCK : (j % 2 + 1) * BLOCK]
            if e > 0:
                next(sums[e - 1])
    for done in sends:
        done.wait_send()
    while sums:
        sums = [one for one in sums if next(one, None) is not None]
    for st, one in zip(P.streams, held):
        g_ref[pl.ds(st.base, st.packed), :] = one[8][...]


def sum_everywhere(P, S, at, where, held):
    (p, rc, rx, hx, ry, hy, rz, gy, o,
     cs, cd, ss, sd, ys, yd, zs, zd, yas, yad, xas, xad, cas, cad) = held
    at_x, at_y, at_z, sibling = at
    z, c, y, x = where

    def half(i):
        return pl.ds(pl.multiple_of(i * S.half, 8), S.half)

    def part(i):
        return pl.ds(pl.multiple_of((c * P.nx + i) * S.part, 8), S.part)

    def piece(i):
        return pl.ds(pl.multiple_of(i * S.piece, 8), S.piece)

    def begin(copies):
        for copy in copies:
            copy.start()
        return copies

    copies = begin([remote(p.at[half(1 - c)], rc, cs.at[0], cd.at[0], sibling)])
    if S.padded > S.part:
        hx[pl.ds(S.part, S.padded - S.part), :] = jnp.zeros((S.padded - S.part, BLOCK), jnp.float32)
    yield True
    copies[0].wait()
    p[half(c), :] = p[half(c), :] + rc[...]

    copies = begin([remote(p.at[part((x + d) % P.nx)], rx.at[d - 1], ss.at[d - 1], sd.at[d - 1], at_x(d))
                    for d in range(1, P.nx)])
    yield True
    total = p[part(x), :]
    for d, copy in enumerate(copies):
        copy.wait()
        total = total + rx[d]
    hx[pl.ds(0, S.part), :] = total

    copies = begin([remote(hx.at[piece((y + d) % P.ny)], ry.at[d - 1], ys.at[d - 1], yd.at[d - 1], at_y(d))
                    for d in range(1, P.ny)])
    yield True
    total = hx[piece(y), :]
    for d, copy in enumerate(copies):
        copy.wait()
        total = total + ry[d]
    hy[...] = total

    copies = begin([remote(hy, rz.at[z], zs.at[d - 1], zd.at[d - 1], at_z(d)) for d in range(1, P.nz)])
    rz[z] = total
    yield True
    for copy in copies:
        copy.wait()
    total = rz[0]
    for i in range(1, P.nz):
        total = total + rz[i]
    gy[piece(y), :] = total

    copies = begin([remote(gy.at[piece(y)], gy.at[piece(y)], yas.at[d - 1], yad.at[d - 1], at_y(d))
                    for d in range(1, P.ny)])
    yield True
    for copy in copies:
        copy.wait()
    copies = begin([remote(gy.at[pl.ds(0, S.part)], o.at[part(x)], xas.at[d - 1], xad.at[d - 1], at_x(d))
                    for d in range(1, P.nx)])
    o[part(x), :] = gy[pl.ds(0, S.part), :]
    yield True
    for copy in copies:
        copy.wait()
    copies = begin([remote(o.at[half(c)], o.at[half(c)], cas.at[0], cad.at[0], sibling)])
    yield True
    copies[0].wait()


def filter_and_gram(plan, weights, record):
    P = plan
    f32, dma = jnp.float32, pltpu.SemaphoreType.DMA
    return pl.pallas_call(
        functools.partial(gather_body, plan),
        out_shape=(
            jax.ShapeDtypeStruct((P.time, P.width), f32),
            jax.ShapeDtypeStruct((len(ORDER) * BLOCK, BLOCK), f32),
        ),
        in_specs=[pl.BlockSpec(memory_space=pltpu.HBM)] * 2,
        out_specs=(pl.BlockSpec(memory_space=pltpu.VMEM),) * 2,
        scratch_shapes=[
            pltpu.SMEM((P.taps,), f32),
            pltpu.VMEM((P.time, P.width), f32),
            pltpu.VMEM((BLOCK, 3 * BLOCK), f32),
            pltpu.VMEM((3, 256, 256), f32),
            dma, dma((P.chunks, P.tm - 1)), dma((P.chunks,)), dma((P.chunks,)),
            *[b for S in P.streams for b in S.buffers(P)],
        ],
        compiler_params=pltpu.CompilerParams(
            collective_id=0, has_side_effects=True, vmem_limit_bytes=48 << 20),
        name="gather_filter_gram",
    )(weights, record)


def solution(mesh):
    def per_device(record, weights):
        rows, width = record.shape[0], record.shape[1] // mesh.shape["tm"]
        plan = Plan(mesh, ALONG_X, rows, width, weights.shape[0])
        fx, gram = filter_and_gram(plan, weights, record)
        points = width * mesh.shape["tm"] * mesh.shape["space"]
        lower, basis = factor_and_solve(gram, fx, points)
        return lower, basis.reshape(plan.time, 1, width)

    return jax.shard_map(
        per_device,
        mesh=mesh,
        in_specs=(P("tm", "space"), P()),
        out_specs=(P(), P(None, "space", "tm")),
        check_vma=False,
    )
```

time: 114 us -> 102 us (0.89)
  Pallas kernels: 112 us -> 99.1 us
    pallas_call x1, Pallas kernels: 27.7 us -> 17.7 us  [factor_and_solve(): pl.pallas_call(functools.partial(body, 1.0 / points), out_shape=(jax.Shap...]
    pallas_call x1, Pallas kernels: 83.9 us -> 81.4 us  [filter_and_gram(): pl.pallas_call(functools.partial(gather_body, plan), out_shape=(jax.Shape...]
where the time goes in v2:
time: 102 us
  Pallas kernels  99.1 us (97%)
  local copies, waits for them, and re-layouts  2.06 us (2%)
    pallas_call x1, Pallas kernels, filter_and_gram(): pl.pallas_call(functools.partial(gather_body, plan), out_shape=(jax.Shape...  81.4 us
    pallas_call x1, Pallas kernels, factor_and_solve(): pl.pallas_call(functools.partial(body, 1.0 / points), out_shape=(jax.Shap...  17.7 us
    unnamed x4, local copies, waits for them, and re-layouts  2.06 us

profile of v2, /device:TPU:1, one launch (start us, length us, event | category | flops | bytes accessed | tf_op | source)
XLA Modules:
  0.0 101.8 jit_solution(15348980087394485571)
XLA Ops:
  0.6 0.0 copy-start
  0.6 1.4 %copy-done = f32[32,12288]{1,0:T(8,128)S(1)} copy-done((f32[32,12288]{1,0:T(8,128)S(1)}, f32[32,12288]{1,0:T(8,128)}, u32[]{:S(2)}) %copy-start) | copy-done | bytes 1572888
  2.0 0.0 copy-start.1
  2.0 0.7 copy-done.1
  2.7 81.4 %gather_filter_gram.1 = (f32[512,768]{1,0:T(8,128)S(1)}, f32[1280,128]{1,0:T(8,128)S(1)}) custom-call(f32[31]{0:T(128)S(1)} %copy-done.1, f32[32,12288]{1,0:T(8,128)S(1)} %copy-done), custom_call_target="tpu_custom_call" | custom-call | tf_op jit(solution)/shard_map/gather_filter_gram/pallas_call | solution.py:369
  84.2 17.7 %factor.1 = (f32[512,512]{1,0:T(8,128)}, f32[3072,128]{1,0:T(8,128)}) custom-call(f32[1280,128]{1,0:T(8,128)S(1)} %get-tuple-element.6.g_ref, f32[512,768]{1,0:T(8,128)S(1)} %get-tuple-element.7.fx_ref), custom_call_target="tpu_custom_call" | custom-call | tf_op jit(solution)/shard_map/factor/pallas_call | solution.py:138
Async XLA Ops:
  0.6 1.4 %copy-start = (f32[32,12288]{1,0:T(8,128)S(1)}, f32[32,12288]{1,0:T(8,128)}, u32[]{:S(2)}) copy-start(f32[32,12288]{1,0:T(8,128)} %x_ref.1) | copy-start | bytes 4718596
  2.0 0.7 copy-start.1

commit v3 on v2

--- a/solution.py
+++ b/solution.py
@@ -162,21 +162,24 @@
 
 
 class Stream:
-    def __init__(self, first, count, plan):
+    def __init__(self, first, count, axes, plan):
+        self.axes = axes
+        n1, n2 = (plan.sizes[axis] for axis in axes)
+        self.n1, self.n2 = n1, n2
         self.base, self.packed = first * BLOCK, count * BLOCK
         self.half = self.packed // 2
-        self.part = self.half // plan.nx
-        self.piece = -(-self.part // (8 * plan.ny)) * 8
-        self.padded = self.piece * plan.ny
+        self.part = self.half // n1
+        self.piece = -(-self.part // (8 * n2)) * 8
+        self.padded = self.piece * n2
 
     def buffers(self, plan):
-        x, y, z = plan.nx - 1, plan.ny - 1, plan.nz - 1
+        u, v, z = self.n1 - 1, self.n2 - 1, plan.nz - 1
         shapes = [
-            (self.packed, BLOCK), (self.half, BLOCK), (x, self.part, BLOCK), (self.padded, BLOCK),
-            (y, self.piece, BLOCK), (self.piece, BLOCK), (plan.nz, self.piece, BLOCK),
+            (self.packed, BLOCK), (self.half, BLOCK), (u, self.part, BLOCK), (self.padded, BLOCK),
+            (v, self.piece, BLOCK), (self.piece, BLOCK), (plan.nz, self.piece, BLOCK),
             (self.padded, BLOCK), (self.packed, BLOCK)]
         dma = pltpu.SemaphoreType.DMA
-        counts = [1, 1, x, x, y, y, z, z, y, y, x, x, 1, 1]
+        counts = [1, 1, u, u, v, v, z, z, v, v, u, u, 1, 1]
         return [pltpu.VMEM(shape, jnp.float32) for shape in shapes] + [dma((n,)) for n in counts]
 
 
@@ -187,7 +190,8 @@
         self.rows, self.width, self.taps = rows, width, taps
         self.time = rows * self.tm
         self.chunks = width // CHUNK
-        self.streams = [Stream(first, count, self) for first, count in ((0, 4), (4, 6))]
+        self.sizes = {"x": self.nx, "y": self.ny}
+        self.streams = [Stream(0, 4, "yx", self), Stream(4, 6, "xy", self)]
 
 
 def remote(src, dst, send, recv, where):
@@ -196,7 +200,7 @@
     )
 
 
-def gather_body(plan, w_hbm, x_ref, fx_ref, g_ref, w_ref, xr, band, acc, ws, xs, xd, xl, *rest):
+def gather_body(plan, w_hbm, x_ref, fx_ref, g_ref, w_ref, xr, band, acc, relay, ws, xs, xd, xl, rs, rd, fs, *rest):
     P = plan
     t, s = lax.axis_index("tm"), lax.axis_index("space")
     z, c = t // 2, t % 2
@@ -227,22 +231,40 @@
         pl.semaphore_signal(barrier, inc=1, device_id=at_y(d), device_id_type=MESH)
     pl.semaphore_wait(barrier, (P.tm - 1) + (P.nx - 1) + (P.ny - 1))
 
-    mine = pl.ds(pl.multiple_of(t * P.rows, 8), P.rows)
-    steps = sorted(range(1, P.tm), key=lambda d: -min(d, P.tm - d))
-    sends, local = [], []
+    far = P.nz // 2
+
+    def theirs(device, h):
+        return x_ref.at[:, pl.ds(pl.multiple_of(device * P.width + h * CHUNK, 128), CHUNK)]
+
+    def block(device, h):
+        return xr.at[pl.ds(pl.multiple_of(device * P.rows, 8), P.rows), pl.ds(h * CHUNK, CHUNK)]
+
+    def device(dz, core):
+        return ((z + dz + P.nz) % P.nz) * 2 + core
+
+    sends, local, relayed = [], [], {}
     for h in range(P.chunks):
-        there = pl.ds(h * CHUNK, CHUNK)
-        for d in steps:
-            peer = (t + d) % P.tm
-            src = x_ref.at[:, pl.ds(pl.multiple_of(peer * P.width + h * CHUNK, 128), CHUNK)]
-            copy = remote(src, xr.at[mine, there], xs.at[h, d - 1], xd.at[h], at_tm(peer))
+        for core, way in enumerate((1, -1)):
+            relayed[core, h] = remote(theirs(device(far, core), h), relay.at[core, h],
+                                      rs.at[core, h], rd.at[core, h], at_tm(device(way, c)))
+            relayed[core, h].start()
+    for h in range(P.chunks):
+        peers = [device(way * dz, core) for dz in range(far - 1, 0, -1) for way in (1, -1) for core in (0, 1)]
+        for n, peer in enumerate(peers + [device(0, 1 - c)]):
+            copy = remote(theirs(peer, h), block(t, h), xs.at[h, n], xd.at[h], at_tm(peer))
             copy.start()
             sends.append(copy)
-        own = pltpu.make_async_copy(
-            x_ref.at[:, pl.ds(pl.multiple_of(t * P.width + h * CHUNK, 128), CHUNK)],
-            xr.at[mine, there], xl.at[h])
+        own = pltpu.make_async_copy(theirs(t, h), block(t, h), xl.at[h])
         own.start()
         local.append(own)
+    for h in range(P.chunks):
+        for core, way in enumerate((1, -1)):
+            relayed[core, h].wait_recv()
+            copy = remote(relay.at[core, h], block(device(-way, c), h), fs.at[core, h], xd.at[h],
+                          at_tm(device(way * (far - 1), core)))
+            copy.start()
+            sends.append(copy)
+    sends.extend(relayed.values())
 
     r = lax.broadcasted_iota(jnp.int32, (BLOCK, 3 * BLOCK), 0)
     q = lax.broadcasted_iota(jnp.int32, (BLOCK, 3 * BLOCK), 1)
@@ -253,9 +275,11 @@
         f = jnp.where(tap == k, w_ref[k], f)
     band[...] = f
 
+    at = {'x': at_x, 'y': at_y, 'z': at_z, 'core': sibling}
+    where = {'x': x, 'y': y, 'z': z, 'core': c}
     size = len(rest) // len(P.streams)
     held = [rest[i * size : (i + 1) * size] for i in range(len(P.streams))]
-    sums = [sum_everywhere(P, S, (at_x, at_y, at_z, sibling), (z, c, y, x), one)
+    sums = [sum_everywhere(P, S, at, where, one)
             for S, one in zip(P.streams, held)]
     nb = P.time // BLOCK
     for h in range(P.chunks):
@@ -295,14 +319,16 @@
 def sum_everywhere(P, S, at, where, held):
     (p, rc, rx, hx, ry, hy, rz, gy, o,
      cs, cd, ss, sd, ys, yd, zs, zd, yas, yad, xas, xad, cas, cad) = held
-    at_x, at_y, at_z, sibling = at
-    z, c, y, x = where
+    at_z, sibling = at['z'], at['core']
+    at_1, at_2 = (at[axis] for axis in S.axes)
+    i1, i2 = (where[axis] for axis in S.axes)
+    z, c = where['z'], where['core']
 
     def half(i):
         return pl.ds(pl.multiple_of(i * S.half, 8), S.half)
 
     def part(i):
-        return pl.ds(pl.multiple_of((c * P.nx + i) * S.part, 8), S.part)
+        return pl.ds(pl.multiple_of((c * S.n1 + i) * S.part, 8), S.part)
 
     def piece(i):
         return pl.ds(pl.multiple_of(i * S.piece, 8), S.piece)
@@ -319,19 +345,19 @@
     copies[0].wait()
     p[half(c), :] = p[half(c), :] + rc[...]
 
-    copies = begin([remote(p.at[part((x + d) % P.nx)], rx.at[d - 1], ss.at[d - 1], sd.at[d - 1], at_x(d))
-                    for d in range(1, P.nx)])
-    yield True
-    total = p[part(x), :]
+    copies = begin([remote(p.at[part((i1 + d) % S.n1)], rx.at[d - 1], ss.at[d - 1], sd.at[d - 1], at_1(d))
+                    for d in range(1, S.n1)])
+    yield True
+    total = p[part(i1), :]
     for d, copy in enumerate(copies):
         copy.wait()
         total = total + rx[d]
     hx[pl.ds(0, S.part), :] = total
 
-    copies = begin([remote(hx.at[piece((y + d) % P.ny)], ry.at[d - 1], ys.at[d - 1], yd.at[d - 1], at_y(d))
-                    for d in range(1, P.ny)])
-    yield True
-    total = hx[piece(y), :]
+    copies = begin([remote(hx.at[piece((i2 + d) % S.n2)], ry.at[d - 1], ys.at[d - 1], yd.at[d - 1], at_2(d))
+                    for d in range(1, S.n2)])
+    yield True
+    total = hx[piece(i2), :]
     for d, copy in enumerate(copies):
         copy.wait()
         total = total + ry[d]
@@ -345,16 +371,16 @@
     total = rz[0]
     for i in range(1, P.nz):
         total = total + rz[i]
-    gy[piece(y), :] = total
-
-    copies = begin([remote(gy.at[piece(y)], gy.at[piece(y)], yas.at[d - 1], yad.at[d - 1], at_y(d))
-                    for d in range(1, P.ny)])
+    gy[piece(i2), :] = total
+
+    copies = begin([remote(gy.at[piece(i2)], gy.at[piece(i2)], yas.at[d - 1], yad.at[d - 1], at_2(d))
+                    for d in range(1, S.n2)])
     yield True
     for copy in copies:
         copy.wait()
-    copies = begin([remote(gy.at[pl.ds(0, S.part)], o.at[part(x)], xas.at[d - 1], xad.at[d - 1], at_x(d))
-                    for d in range(1, P.nx)])
-    o[part(x), :] = gy[pl.ds(0, S.part), :]
+    copies = begin([remote(gy.at[pl.ds(0, S.part)], o.at[part(i1)], xas.at[d - 1], xad.at[d - 1], at_1(d))
+                    for d in range(1, S.n1)])
+    o[part(i1), :] = gy[pl.ds(0, S.part), :]
     yield True
     for copy in copies:
         copy.wait()
@@ -379,11 +405,13 @@
             pltpu.VMEM((P.time, P.width), f32),
             pltpu.VMEM((BLOCK, 3 * BLOCK), f32),
             pltpu.VMEM((3, 256, 256), f32),
-            dma, dma((P.chunks, P.tm - 1)), dma((P.chunks,)), dma((P.chunks,)),
+            pltpu.VMEM((2, P.chunks, P.rows, CHUNK), f32),
+            dma, dma((P.chunks, P.tm - 3)), dma((P.chunks,)), dma((P.chunks,)),
+            *[dma((2, P.chunks))] * 3,
             *[b for S in P.streams for b in S.buffers(P)],
         ],
         compiler_params=pltpu.CompilerParams(
-            collective_id=0, has_side_effects=True, vmem_limit_bytes=48 << 20),
+            collective_id=0, has_side_effects=True, vmem_limit_bytes=52000 << 10),
         name="gather_filter_gram",
     )(weights, record)
 

time: 102 us -> 105 us (1.029)
  Pallas kernels: 99.1 us -> 104 us
  local copies, waits for them, and re-layouts: 2.06 us -> 0.65 us
    pallas_call x1, Pallas kernels: 81.4 us -> 86 us  [filter_and_gram(): pl.pallas_call(functools.partial(gather_body, plan), out_shape=(jax.Shape...]
    unnamed x4 -> x2, local copies, waits for them, and re-layouts: 2.06 us -> 0.65 us
where the time goes in v3:
time: 105 us
  Pallas kernels  104 us (99%)
    pallas_call x1, Pallas kernels, filter_and_gram(): pl.pallas_call(functools.partial(gather_body, plan), out_shape=(jax.Shape...  86 us
    pallas_call x1, Pallas kernels, factor_and_solve(): pl.pallas_call(functools.partial(body, 1.0 / points), out_shape=(jax.Shap...  17.7 us

profile of v3, /device:TPU:1, one launch (start us, length us, event | category | flops | bytes accessed | tf_op | source)
XLA Modules:
  0.0 105.0 jit_solution(4486802617929420283)
XLA Ops:
  0.6 0.0 copy-start
  0.6 0.6 copy-done
  1.3 86.0 %gather_filter_gram.1 = (f32[512,768]{1,0:T(8,128)S(1)}, f32[1280,128]{1,0:T(8,128)S(1)}) custom-call(f32[31]{0:T(128)S(1)} %copy-done, f32[32,12288]{1,0:T(8,128)} %x_ref.1), custom_call_target="tpu_custom_call" | custom-call | tf_op jit(solution)/shard_map/gather_filter_gram/pallas_call | solution.py:395
  87.3 17.7 %factor.1 = (f32[512,512]{1,0:T(8,128)}, f32[3072,128]{1,0:T(8,128)}) custom-call(f32[1280,128]{1,0:T(8,128)S(1)} %get-tuple-element.6.g_ref, f32[512,768]{1,0:T(8,128)S(1)} %get-tuple-element.7.fx_ref), custom_call_target="tpu_custom_call" | custom-call | tf_op jit(solution)/shard_map/factor/pallas_call | solution.py:138
Async XLA Ops:
  0.6 0.7 copy-start

commit v4 on v2

--- a/solution.py
+++ b/solution.py
@@ -94,7 +94,7 @@
     return upper, inverse
 
 
-def body(scale, g_ref, fx_ref, l_ref, y_ref, a, u, t, f, cs, gs):
+def body(scale, g_ref, fx_ref, l_out, y_out, a, u, t, f, cs, gs, l_ref, y_ref, sem):
     eye = lax.broadcasted_iota(jnp.int32, (B, B), 0) == lax.broadcasted_iota(jnp.int32, (B, B), 1)
     across, down, root = [], [], []
     for k in range(4):
@@ -109,6 +109,7 @@
             a[b] = (g_ref[pl.ds(b * B, B), :] * scale) * down[i] * across[k]
         f[pl.ds(k * B, B), :] = fx_ref[pl.ds(k * B, B), :] * down[k]
     l_ref[...] = jnp.zeros_like(l_ref)
+    copies = []
     for k in range(4):
         d = OFF[k]
         rows = [a[d, pl.ds(8 * v, 8), :] for v in range(16)]
@@ -132,6 +133,17 @@
         for q in range(wide):
             y_ref[pl.ds(k * B * wide + q, B, stride=wide), :] = y[:, q * B : (q + 1) * B]
 
+        strip = pl.ds(k * B, B)
+        wide = f.shape[1] // B
+        for e, (here, there) in enumerate((
+                (l_ref.at[strip], l_out.at[strip]),
+                (y_ref.at[pl.ds(k * B * wide, B * wide)], y_out.at[pl.ds(k * B * wide, B * wide)]))):
+            copy = pltpu.make_async_copy(here, there, sem.at[e, k])
+            copy.start()
+            copies.append(copy)
+    for copy in copies:
+        copy.wait()
+
 
 def factor_and_solve(gram, fx, points):
     rows, cols = fx.shape
@@ -142,7 +154,7 @@
             jax.ShapeDtypeStruct((rows * cols // B, B), jnp.float32),
         ),
         in_specs=[pl.BlockSpec(memory_space=pltpu.VMEM)] * 2,
-        out_specs=(pl.BlockSpec(memory_space=pltpu.VMEM),) * 2,
+        out_specs=(pl.BlockSpec(memory_space=pl.ANY),) * 2,
         scratch_shapes=[
             pltpu.VMEM((10, B, B), jnp.float32),
             pltpu.VMEM((B, B), jnp.float32),
@@ -150,6 +162,9 @@
             pltpu.VMEM((rows, cols), jnp.float32),
             pltpu.VMEM((2, 8, 8, B), jnp.float32),
             pltpu.VMEM((2, 8, B), jnp.float32),
+            pltpu.VMEM((rows, rows), jnp.float32),
+            pltpu.VMEM((rows * cols // B, B), jnp.float32),
+            pltpu.SemaphoreType.DMA((2, 4)),
         ],
         compiler_params=pltpu.CompilerParams(vmem_limit_bytes=48 << 20),
         name="factor",
@@ -158,6 +173,8 @@
 
 BLOCK = 128
 CHUNK = 256
+STREAMS = ((0, 4), (4, 3), (7, 3))
+READY = ((), (0, 1), (2,))
 ORDER = ((0, 0), (1, 0), (2, 0), (3, 0), (1, 1), (2, 1), (3, 1), (2, 2), (3, 2), (3, 3))
 
 
@@ -187,7 +204,7 @@
         self.rows, self.width, self.taps = rows, width, taps
         self.time = rows * self.tm
         self.chunks = width // CHUNK
-        self.streams = [Stream(first, count, self) for first, count in ((0, 4), (4, 6))]
+        self.streams = [Stream(first, count, self) for first, count in STREAMS]
 
 
 def remote(src, dst, send, recv, where):
@@ -196,7 +213,7 @@
     )
 
 
-def gather_body(plan, w_hbm, x_ref, fx_ref, g_ref, w_ref, xr, band, acc, ws, xs, xd, xl, *rest):
+def gather_body(plan, w_hbm, x_ref, fx_out, g_ref, w_ref, fx_ref, fs, xr, band, acc, ws, xs, xd, xl, *rest):
     P = plan
     t, s = lax.axis_index("tm"), lax.axis_index("space")
     z, c = t // 2, t % 2
@@ -257,6 +274,7 @@
     held = [rest[i * size : (i + 1) * size] for i in range(len(P.streams))]
     sums = [sum_everywhere(P, S, (at_x, at_y, at_z, sibling), (z, c, y, x), one)
             for S, one in zip(P.streams, held)]
+    leaving = []
     nb = P.time // BLOCK
     for h in range(P.chunks):
         there = pl.ds(h * CHUNK, CHUNK)
@@ -268,6 +286,9 @@
             fx_ref[pl.ds(i * BLOCK, BLOCK), there] = dot(
                 band[:, (lo - i + 1) * BLOCK : (hi - i + 1) * BLOCK],
                 xr[pl.ds(lo * BLOCK, (hi - lo) * BLOCK), there])
+        copy = pltpu.make_async_copy(fx_ref.at[:, there], fx_out.at[:, there], fs.at[h])
+        copy.start()
+        leaving.append(copy)
         top = fx_ref[pl.ds(0, 256), there]
         low = fx_ref[pl.ds(256, 256), there]
         for e, (u, v) in enumerate(((top, top), (low, top), (low, low))):
@@ -279,15 +300,20 @@
                 continue
             for n, (i, j) in enumerate(ORDER):
                 if ((0, 0), (1, 0), (1, 1))[e] == (i // 2, j // 2):
-                    st = 0 if n < 4 else 1
+                    st = max(o for o, S in enumerate(P.streams) if S.base <= n * BLOCK)
                     held[st][0][pl.ds(n * BLOCK - P.streams[st].base, BLOCK), :] = new[
                         (i % 2) * BLOCK : (i % 2 + 1) * BLOCK, (j % 2) * BLOCK : (j % 2 + 1) * BLOCK]
-            if e > 0:
-                next(sums[e - 1])
-    for done in sends:
-        done.wait_send()
+            for o in READY[e]:
+                next(sums[o])
+    phase = 0
     while sums:
         sums = [one for one in sums if next(one, None) is not None]
+        phase += 1
+        if phase == 2:
+            for done in sends:
+                done.wait_send()
+            for copy in leaving:
+                copy.wait()
     for st, one in zip(P.streams, held):
         g_ref[pl.ds(st.base, st.packed), :] = one[8][...]
 
@@ -298,6 +324,8 @@
     at_x, at_y, at_z, sibling = at
     z, c, y, x = where
 
+    begun = []
+
     def half(i):
         return pl.ds(pl.multiple_of(i * S.half, 8), S.half)
 
@@ -310,13 +338,16 @@
     def begin(copies):
         for copy in copies:
             copy.start()
+        while begun:
+            begun.pop().wait_send()
+        begun.extend(copies)
         return copies
 
     copies = begin([remote(p.at[half(1 - c)], rc, cs.at[0], cd.at[0], sibling)])
     if S.padded > S.part:
         hx[pl.ds(S.part, S.padded - S.part), :] = jnp.zeros((S.padded - S.part, BLOCK), jnp.float32)
     yield True
-    copies[0].wait()
+    copies[0].wait_recv()
     p[half(c), :] = p[half(c), :] + rc[...]
 
     copies = begin([remote(p.at[part((x + d) % P.nx)], rx.at[d - 1], ss.at[d - 1], sd.at[d - 1], at_x(d))
@@ -324,7 +355,7 @@
     yield True
     total = p[part(x), :]
     for d, copy in enumerate(copies):
-        copy.wait()
+        copy.wait_recv()
         total = total + rx[d]
     hx[pl.ds(0, S.part), :] = total
 
@@ -333,7 +364,7 @@
     yield True
     total = hx[piece(y), :]
     for d, copy in enumerate(copies):
-        copy.wait()
+        copy.wait_recv()
         total = total + ry[d]
     hy[...] = total
 
@@ -341,7 +372,7 @@
     rz[z] = total
     yield True
     for copy in copies:
-        copy.wait()
+        copy.wait_recv()
     total = rz[0]
     for i in range(1, P.nz):
         total = total + rz[i]
@@ -351,16 +382,18 @@
                     for d in range(1, P.ny)])
     yield True
     for copy in copies:
-        copy.wait()
+        copy.wait_recv()
     copies = begin([remote(gy.at[pl.ds(0, S.part)], o.at[part(x)], xas.at[d - 1], xad.at[d - 1], at_x(d))
                     for d in range(1, P.nx)])
     o[part(x), :] = gy[pl.ds(0, S.part), :]
     yield True
     for copy in copies:
-        copy.wait()
+        copy.wait_recv()
     copies = begin([remote(o.at[half(c)], o.at[half(c)], cas.at[0], cad.at[0], sibling)])
     yield True
-    copies[0].wait()
+    copies[0].wait_recv()
+    for copy in begun:
+        copy.wait_send()
 
 
 def filter_and_gram(plan, weights, record):
@@ -373,9 +406,11 @@
             jax.ShapeDtypeStruct((len(ORDER) * BLOCK, BLOCK), f32),
         ),
         in_specs=[pl.BlockSpec(memory_space=pltpu.HBM)] * 2,
-        out_specs=(pl.BlockSpec(memory_space=pltpu.VMEM),) * 2,
+        out_specs=(pl.BlockSpec(memory_space=pl.ANY), pl.BlockSpec(memory_space=pltpu.VMEM)),
         scratch_shapes=[
             pltpu.SMEM((P.taps,), f32),
+            pltpu.VMEM((P.time, P.width), f32),
+            dma((P.chunks,)),
             pltpu.VMEM((P.time, P.width), f32),
             pltpu.VMEM((BLOCK, 3 * BLOCK), f32),
             pltpu.VMEM((3, 256, 256), f32),
@@ -383,7 +418,7 @@
             *[b for S in P.streams for b in S.buffers(P)],
         ],
         compiler_params=pltpu.CompilerParams(
-            collective_id=0, has_side_effects=True, vmem_limit_bytes=48 << 20),
+            collective_id=0, has_side_effects=True, vmem_limit_bytes=52000 << 10),
         name="gather_filter_gram",
     )(weights, record)
 

time: 102 us -> 100 us (0.980)
  local copies, waits for them, and re-layouts: 2.06 us -> 0.65 us
    unnamed x4 -> x2, local copies, waits for them, and re-layouts: 2.06 us -> 0.65 us
where the time goes in v4:
time: 100 us; the launch traced here: 99.8 us
  Pallas kernels  98.4 us (98%)
    pallas_call x1, Pallas kernels, filter_and_gram(): pl.pallas_call(functools.partial(gather_body, plan), out_shape=(jax.Shape...  80.9 us
    pallas_call x1, Pallas kernels, factor_and_solve(): pl.pallas_call(functools.partial(body, 1.0 / points), out_shape=(jax.Shap...  17.5 us

profile of v4, /device:TPU:1, one launch (start us, length us, event | category | flops | bytes accessed | tf_op | source)
XLA Modules:
  0.0 99.8 jit_solution(9577875943895227046)
XLA Ops:
  0.6 0.0 copy-start
  0.6 0.6 copy-done
  1.3 80.9 %gather_filter_gram.1 = (f32[512,768]{1,0:T(8,128)S(1)}, f32[1280,128]{1,0:T(8,128)S(1)}) custom-call(f32[31]{0:T(128)S(1)} %copy-done, f32[32,12288]{1,0:T(8,128)} %x_ref.1), custom_call_target="tpu_custom_call" | custom-call | tf_op jit(solution)/shard_map/gather_filter_gram/pallas_call | solution.py:402
  82.2 17.5 %factor.1 = (f32[512,512]{1,0:T(8,128)}, f32[3072,128]{1,0:T(8,128)}) custom-call(f32[1280,128]{1,0:T(8,128)S(1)} %get-tuple-element.6.g_ref, f32[512,768]{1,0:T(8,128)S(1)} %get-tuple-element.7.fx_ref), custom_call_target="tpu_custom_call" | custom-call | tf_op jit(solution)/shard_map/factor/pallas_call | solution.py:150
Async XLA Ops:
  0.6 0.7 copy-start

commit v5 on v4

--- a/solution.py
+++ b/solution.py
@@ -110,6 +110,15 @@
         f[pl.ds(k * B, B), :] = fx_ref[pl.ds(k * B, B), :] * down[k]
     l_ref[...] = jnp.zeros_like(l_ref)
     copies = []
+    wide = f.shape[1] // B
+
+    def leave(k):
+        strip, lines = pl.ds(k * B, B), pl.ds(k * B * wide, B * wide)
+        for e, (here, there) in enumerate(((l_ref.at[strip], l_out.at[strip]), (y_ref.at[lines], y_out.at[lines]))):
+            copy = pltpu.make_async_copy(here, there, sem.at[e, k])
+            copy.start()
+            copies.append(copy)
+
     for k in range(4):
         d = OFF[k]
         rows = [a[d, pl.ds(8 * v, 8), :] for v in range(16)]
@@ -118,6 +127,8 @@
             u[pl.ds(8 * v, 8), :] = up[v]
             t[pl.ds(8 * v, 8), :] = iv[v]
         tk = t[...]
+        if k > 0:
+            leave(k - 1)
         l_ref[pl.ds(k * B, B), pl.ds(k * B, B)] = u[...].T * root[k]
         low = {}
         for i in range(k + 1, 4):
@@ -133,14 +144,7 @@
         for q in range(wide):
             y_ref[pl.ds(k * B * wide + q, B, stride=wide), :] = y[:, q * B : (q + 1) * B]
 
-        strip = pl.ds(k * B, B)
-        wide = f.shape[1] // B
-        for e, (here, there) in enumerate((
-                (l_ref.at[strip], l_out.at[strip]),
-                (y_ref.at[pl.ds(k * B * wide, B * wide)], y_out.at[pl.ds(k * B * wide, B * wide)]))):
-            copy = pltpu.make_async_copy(here, there, sem.at[e, k])
-            copy.start()
-            copies.append(copy)
+    leave(3)
     for copy in copies:
         copy.wait()
 
@@ -193,7 +197,7 @@
             (y, self.piece, BLOCK), (self.piece, BLOCK), (plan.nz, self.piece, BLOCK),
             (self.padded, BLOCK), (self.packed, BLOCK)]
         dma = pltpu.SemaphoreType.DMA
-        counts = [1, 1, x, x, y, y, z, z, y, y, x, x, 1, 1]
+        counts = [plan.nx, plan.nx, x, x, y, y, z, z, y, y, x, x, plan.nx, plan.nx]
         return [pltpu.VMEM(shape, jnp.float32) for shape in shapes] + [dma((n,)) for n in counts]
 
 
@@ -326,11 +330,8 @@
 
     begun = []
 
-    def half(i):
-        return pl.ds(pl.multiple_of(i * S.half, 8), S.half)
-
-    def part(i):
-        return pl.ds(pl.multiple_of((c * P.nx + i) * S.part, 8), S.part)
+    def part(i, core):
+        return pl.ds(pl.multiple_of((core * P.nx + i) * S.part, 8), S.part)
 
     def piece(i):
         return pl.ds(pl.multiple_of(i * S.piece, 8), S.piece)
@@ -338,22 +339,32 @@
     def begin(copies):
         for copy in copies:
             copy.start()
+        return went(copies)
+
+    def went(copies):
         while begun:
             begun.pop().wait_send()
         begun.extend(copies)
         return copies
 
-    copies = begin([remote(p.at[half(1 - c)], rc, cs.at[0], cd.at[0], sibling)])
+    order = (*range(1, P.nx), 0)
+    copies = begin([remote(p.at[part((x + d) % P.nx, 1 - c)], rc.at[pl.ds(d * S.part, S.part)],
+                           cs.at[d], cd.at[d], sibling) for d in order])
     if S.padded > S.part:
         hx[pl.ds(S.part, S.padded - S.part), :] = jnp.zeros((S.padded - S.part, BLOCK), jnp.float32)
     yield True
-    copies[0].wait_recv()
-    p[half(c), :] = p[half(c), :] + rc[...]
-
-    copies = begin([remote(p.at[part((x + d) % P.nx)], rx.at[d - 1], ss.at[d - 1], sd.at[d - 1], at_x(d))
-                    for d in range(1, P.nx)])
-    yield True
-    total = p[part(x), :]
+
+    onward = []
+    for d, copy in zip(order, copies):
+        copy.wait_recv()
+        kept = part((x + d) % P.nx, c)
+        p[kept, :] = p[kept, :] + rc[pl.ds(d * S.part, S.part), :]
+        if d > 0:
+            onward.append(remote(p.at[kept], rx.at[d - 1], ss.at[d - 1], sd.at[d - 1], at_x(d)))
+            onward[-1].start()
+    copies = went(onward)
+    yield True
+    total = p[part(x, c), :]
     for d, copy in enumerate(copies):
         copy.wait_recv()
         total = total + rx[d]
@@ -383,15 +394,21 @@
     yield True
     for copy in copies:
         copy.wait_recv()
-    copies = begin([remote(gy.at[pl.ds(0, S.part)], o.at[part(x)], xas.at[d - 1], xad.at[d - 1], at_x(d))
+    copies = begin([remote(gy.at[pl.ds(0, S.part)], o.at[part(x, c)], xas.at[d - 1], xad.at[d - 1], at_x(d))
                     for d in range(1, P.nx)])
-    o[part(x), :] = gy[pl.ds(0, S.part), :]
+    o[part(x, c), :] = gy[pl.ds(0, S.part), :]
+    onward = [remote(o.at[part(x, c)], o.at[part(x, c)], cas.at[0], cad.at[0], sibling)]
+    onward[0].start()
+    yield True
+    for d, copy in enumerate(copies, 1):
+        copy.wait_recv()
+        came = o.at[part((x + P.nx - d) % P.nx, c)]
+        onward.append(remote(came, came, cas.at[d], cad.at[d], sibling))
+        onward[-1].start()
+    copies = went(onward)
     yield True
     for copy in copies:
         copy.wait_recv()
-    copies = begin([remote(o.at[half(c)], o.at[half(c)], cas.at[0], cad.at[0], sibling)])
-    yield True
-    copies[0].wait_recv()
     for copy in begun:
         copy.wait_send()
 

time: 100 us -> 100 us (level)
  no operation moved by 1% of the time
where the time goes in v5:
time: 100 us
  Pallas kernels  98.7 us (99%)
    pallas_call x1, Pallas kernels, filter_and_gram(): pl.pallas_call(functools.partial(gather_body, plan), out_shape=(jax.Shape...  81.2 us
    pallas_call x1, Pallas kernels, factor_and_solve(): pl.pallas_call(functools.partial(body, 1.0 / points), out_shape=(jax.Shap...  17.4 us

profile of v5, /device:TPU:1, one launch (start us, length us, event | category | flops | bytes accessed | tf_op | source)
XLA Modules:
  0.0 100.1 jit_solution(16965334577424954458)
XLA Ops:
  0.6 0.0 copy-start
  0.6 0.6 copy-done
  1.3 81.2 %gather_filter_gram.1 = (f32[512,768]{1,0:T(8,128)S(1)}, f32[1280,128]{1,0:T(8,128)S(1)}) custom-call(f32[31]{0:T(128)S(1)} %copy-done, f32[32,12288]{1,0:T(8,128)} %x_ref.1), custom_call_target="tpu_custom_call" | custom-call | tf_op jit(solution)/shard_map/gather_filter_gram/pallas_call | solution.py:419
  82.5 17.4 %factor.1 = (f32[512,512]{1,0:T(8,128)}, f32[3072,128]{1,0:T(8,128)}) custom-call(f32[1280,128]{1,0:T(8,128)S(1)} %get-tuple-element.6.g_ref, f32[512,768]{1,0:T(8,128)S(1)} %get-tuple-element.7.fx_ref), custom_call_target="tpu_custom_call" | custom-call | tf_op jit(solution)/shard_map/factor/pallas_call | solution.py:154
Async XLA Ops:
  0.6 0.7 copy-start
